TPU v7x, 256 devices: a whole 4x4x8 slice. The times are simulated.
256 devices in a mesh: pair: 64 (over z_hi, y, x, core), sec: 4 (over z_lo).
Axes of the slice: x: 4, y: 4, z: 8 (z_hi: 2, z_lo: 4; z = z_hi * 4 + z_lo), core: 2. Of those that a mesh axis runs over, the one named last changes fastest.
Arguments:
- normal_ops: float32 [2, 128, 128, 512], P(None, 'pair', None, 'sec'), may hold values from -6 to 6
- integrals: float32 [2, 64, 128], P(None, 'pair'), may hold values from -1.5 to 1.5
- site_terms: float32 [2, 64, 4, 4], P(None, 'pair'), may hold values from -8 to 8
- basis: float32 [2, 4, 512, 512], P(None, None, None, 'sec'), may hold values from -0.25 to 0.25
Outputs:
- new_normal: float32 [2, 128, 4, 128, 512], P(None, 'pair', None, None, 'sec')
- new_comp: float32 [2, 64, 4, 128, 512], P(None, 'pair', None, None, 'sec')
All inputs are finite; a program needn't handle non-finite values.
Results may differ from a plain program's by a relative error of at most 0.00007.
Values sent between devices are 32-bit elements; how exact they have to be, the bound alone decides.
A program may use at most 64 MiB of HBM per device.

v0:
```python
import jax
import jax.numpy as jnp
from jax import lax
from jax.experimental import pallas as pl
from jax.experimental.pallas import tpu as pltpu
from jax.sharding import PartitionSpec as P

MESH = pl.DeviceIdType.MESH
F32 = jnp.float32
BF16 = jnp.bfloat16
RIGHT, LEFT = 0, 1


def split(x):
    high = x.astype(BF16)
    return high, (x - high.astype(F32)).astype(BF16)


def kernel(
    n_ref, i_ref, t_ref, b_hbm, on_ref, oc_ref,
    bas, bhi, blo, nall, rows, coef, part, done, ochain, xchain,
    b_sem, n_s, n_r, f_s, f_r, c_s, c_r, iz_s, iz_r, ip_s, ip_r, k_s, k_r, o_s, o_r, x_s, x_r,
):
    p = lax.axis_index("pair")
    s = lax.axis_index("sec")
    half = p // 32
    chip = (p // 2) % 16
    core = p % 2
    pairing = s // 2
    odd = s % 2

    def on_chip(q):
        return (half * 32 + q * 2 + core, s)

    mate = (p - core + (1 - core), s)
    z_up = ((p + 32 * ((s + 1) // 4)) % 64, (s + 1) % 4)
    z_down = ((p + 32 * ((4 - s) // 4)) % 64, (s + 3) % 4)
    z_to = (z_up, z_down)

    def remote(src, dst, send, recv, to):
        return pltpu.make_async_remote_copy(
            src_ref=src, dst_ref=dst, send_sem=send, recv_sem=recv, device_id=to, device_id_type=MESH
        )

    def wait_for(ref, sem):
        pltpu.make_async_copy(ref, ref, sem).wait()

    basis_copy = pltpu.make_async_copy(b_hbm, bas, b_sem)
    basis_copy.start()

    re = jnp.broadcast_to(i_ref[0], (8, 128))
    im = jnp.broadcast_to(i_ref[1], (8, 128))
    re_t, im_t = pltpu.roll(re, 64, 1), pltpu.roll(im, 64, 1)
    low = lax.broadcasted_iota(jnp.int32, (8, 128), 1) < 64
    row = lax.broadcasted_iota(jnp.int32, (8, 128), 0)
    tile = jnp.where(
        row == 0,
        jnp.where(low, re, -im_t),
        jnp.where(
            row == 1,
            jnp.where(low, im, re_t),
            jnp.where(row == 2, jnp.where(low, re_t, -im), jnp.where(low, im_t, re)),
        ),
    )
    coef[half, chip] = tile

    barrier = pltpu.get_barrier_semaphore()

    @pl.loop(1, 16)
    def _(d):
        pl.semaphore_signal(barrier, inc=1, device_id=on_chip((chip + d) % 16), device_id_type=MESH)

    for to in (mate, z_up, z_down):
        pl.semaphore_signal(barrier, inc=1, device_id=to, device_id_type=MESH)
    pl.semaphore_wait(barrier, 18)

    def n_slot(way, k):
        return s - k if way == RIGHT else s + k

    def n_can_send(way, k):
        return (s < 3) & (s >= k) if way == RIGHT else (s > 0) & (s + k <= 3)

    def n_can_recv(way, k):
        return s - 1 >= k if way == RIGHT else s + 1 + k <= 3

    def n_copy(way, k, ch):
        slot = n_slot(way, k)
        src = n_ref.at[ch] if k == 0 else nall.at[slot, ch]
        return remote(src, nall.at[slot, ch], n_s.at[way, k, ch], n_r.at[way, k, ch], z_to[way])

    def n_send(way, k, ch):
        @pl.when(n_can_send(way, k))
        def _():
            n_copy(way, k, ch).start()

    def n_wait(way, k, ch):
        @pl.when(n_can_recv(way, k))
        def _():
            wait_for(nall.at[n_slot(way, k + 1), ch], n_r.at[way, k, ch])

    for ch in range(2):
        for way in (RIGHT, LEFT):
            n_send(way, 0, ch)

    def forward(inv, src):
        @pl.loop(1, 16)
        def _(d):
            q = (chip + d) % 16
            remote(src.at[:, :, q], rows.at[inv, :, chip, core], f_s.at[inv], f_r.at[inv], on_chip(q)).start()

        rows[inv, :, chip, core] = src[:, :, chip]

    forward(0, n_ref)

    @pl.when(s == 3)
    def _():
        remote(coef.at[half, chip], coef.at[half, chip], iz_s, iz_r, z_up).start()

    @pl.when(s == 0)
    def _():
        remote(coef.at[half, chip], coef.at[half, chip], iz_s, iz_r, z_down).start()

    basis_copy.wait()
    for g in range(4):
        for r in range(2):
            for a in range(4):
                high, rest = split(bas[r, a, pl.ds(128 * g, 128)])
                bhi[g, pl.ds(128 * r, 128), pl.ds(128 * a, 128)] = high
                blo[g, pl.ds(128 * r, 128), pl.ds(128 * a, 128)] = rest

    wait_for(coef.at[1 - half, chip], iz_r)

    @pl.when(s == 0)
    def _():
        remote(coef.at[1 - half, chip], coef.at[1 - half, chip], iz_s, iz_r, z_up).start()

    @pl.when(s == 3)
    def _():
        remote(coef.at[1 - half, chip], coef.at[1 - half, chip], iz_s, iz_r, z_down).start()

    @pl.loop(1, 16)
    def _(d):
        remote(coef.at[:, chip], coef.at[:, chip], ip_s, ip_r, on_chip((chip + d) % 16)).start()

    def product(real, imag, g):
        top = split(jnp.concatenate([real, -imag], axis=1))
        bottom = split(jnp.concatenate([imag, real], axis=1))
        out = []
        for high, rest in (top, bottom):
            for pair in range(2):
                cols = pl.ds(256 * pair, 256)
                b_high, b_rest = bhi[g, :, cols], blo[g, :, cols]
                dot = lambda x, y: jnp.dot(x, y, preferred_element_type=F32)
                out.append(dot(high, b_high) + (dot(high, b_rest) + dot(rest, b_high)))
        return out

    def renorm_normal(src, g, first=False):
        for j in range(2):
            real = src[0, j].reshape(128, 128)
            imag = src[1, j].reshape(128, 128)
            res = product(real, imag, g)
            for r in range(2):
                for a in range(4):
                    value = res[2 * r + a // 2][:, 128 * (a % 2) : 128 * (a % 2) + 128]
                    if first:
                        on_ref[r, j, a] = value
                    else:
                        on_ref[r, j, a] += value

    def renorm_comp(real, imag, g):
        res = product(real.reshape(128, 128), imag.reshape(128, 128), g)
        for r in range(2):
            for a in range(4):
                oc_ref[r, 0, a] += res[2 * r + a // 2][:, 128 * (a % 2) : 128 * (a % 2) + 128]

    renorm_normal(n_ref, s, first=True)

    for a in range(4):
        real = jnp.zeros((128, 128), F32)
        imag = jnp.zeros((128, 128), F32)
        for b in range(4):
            t_re, t_im = t_ref[0, 0, a, b], t_ref[1, 0, a, b]
            b_re, b_im = bas[0, b, pl.ds(0, 128)], bas[1, b, pl.ds(0, 128)]
            real += t_re * b_re - t_im * b_im
            imag += t_re * b_im + t_im * b_re
        oc_ref[0, 0, a] = real
        oc_ref[1, 0, a] = imag

    def swap(inv):
        wait_for(rows.at[inv, :, pl.ds(0, 15), 0], f_r.at[inv])
        remote(rows.at[inv, :, :, core], rows.at[inv, :, :, core], c_s.at[inv], c_r.at[inv], mate).start()

    def complementary(inv):
        wait_for(rows.at[inv, :, :, 1 - core], c_r.at[inv])
        flat = rows.at[inv].reshape(1024, 128)
        table = coef.reshape(256, 128)
        lines = [table[pl.ds(i, 32, stride=8), :] for i in range(4)]
        left = jnp.concatenate(
            [jnp.where(half == 0, lines[0], lines[2]), jnp.where(half == 0, lines[1], lines[3])], axis=0
        )
        out = part.at[inv].reshape(512, 128)
        for i in range(8):
            res = jnp.dot(left, flat[pl.ds(i, 128, stride=8), :], preferred_element_type=F32, precision=lax.Precision.HIGHEST)
            out[pl.ds(i, 64, stride=8), :] = res

    def back(inv, gi):
        @pl.loop(1, 16)
        def _(d):
            q = (chip + d) % 16
            remote(part.at[inv, :, :, q], done.at[gi, :, :, chip], k_s.at[inv], k_r.at[inv], on_chip(q)).start()

        done[gi, :, :, chip] = part[inv, :, :, chip]

    def wait_back(inv, gi):
        wait_for(done.at[gi, :, :, pl.ds(0, 15)], k_r.at[inv])

    def x_group(way, t):
        return 3 - t if way == RIGHT else t

    def x_copy(way, t, ch, origin):
        g = x_group(way, t)
        src = done.at[g % 2, ch, 1 - half] if origin else xchain.at[g, ch]
        return remote(src, xchain.at[g, ch], x_s.at[way, t, ch], x_r.at[way, t, ch], z_to[way])

    def o_copy(way, t, ch, origin):
        gi = 1 - t if way == RIGHT else t
        src = done.at[gi, ch, half] if origin else ochain.at[gi, ch]
        return remote(src, ochain.at[gi, ch], o_s.at[way, t, ch], o_r.at[t, ch], z_to[way])

    def originate(t):
        for ch in range(2):
            @pl.when(s == 3)
            def _():
                x_copy(RIGHT, t, ch, True).start()

            @pl.when(s == 0)
            def _():
                x_copy(LEFT, t, ch, True).start()

            @pl.when(s == 1)
            def _():
                o_copy(RIGHT, t, ch, True).start()

            @pl.when(s == 2)
            def _():
                o_copy(LEFT, t, ch, True).start()

    def x_take(way, t, ch):
        wait_for(xchain.at[x_group(way, t), ch], x_r.at[way, t, ch])

        @pl.when(s < 3 if way == RIGHT else s > 0)
        def _():
            x_copy(way, t, ch, False).start()

    def o_take(t, ch):
        @pl.when(s < 2)
        def _():
            wait_for(ochain.at[t, ch], o_r.at[t, ch])

            @pl.when(s == 1)
            def _():
                o_copy(LEFT, t, ch, False).start()

        @pl.when(s >= 2)
        def _():
            wait_for(ochain.at[1 - t, ch], o_r.at[t, ch])

            @pl.when(s == 2)
            def _():
                o_copy(RIGHT, t, ch, False).start()

    def near(t):
        for ch in range(2):
            @pl.when(s < 2)
            def _():
                x_take(RIGHT, t, ch)

            @pl.when(s >= 2)
            def _():
                x_take(LEFT, t, ch)

    def far(t):
        for ch in range(2):
            @pl.when(s < 2)
            def _():
                x_take(LEFT, t, ch)

            @pl.when(s >= 2)
            def _():
                x_take(RIGHT, t, ch)

    def n_step(k):
        for ch in range(2):
            for way in (RIGHT, LEFT):
                n_wait(way, k, ch)
                if k < 2:
                    n_send(way, k + 1, ch)

    def n_renorm(k):
        for way in (RIGHT, LEFT):
            @pl.when(n_can_recv(way, k))
            def _():
                slot = n_slot(way, k + 1)
                renorm_normal(nall.at[slot], slot)

    other = s + 1 - 2 * odd
    swap(0)
    n_step(0)
    forward(1, nall.at[other])
    wait_for(coef.at[:, pl.ds(0, 15)], ip_r)
    complementary(0)
    back(0, odd)
    n_renorm(0)
    swap(1)
    n_step(1)
    wait_back(0, odd)
    originate(0)
    complementary(1)
    back(1, 1 - odd)
    n_renorm(1)
    near(0)
    for ch in range(2):
        o_take(0, ch)
    n_step(2)
    wait_back(1, 1 - odd)
    originate(1)
    n_renorm(2)
    far(0)
    near(1)
    for ch in range(2):
        o_take(1, ch)
    far(1)
    for gi in range(2):
        g = 2 * pairing + gi
        renorm_comp(done[gi, 0, half] + xchain[g, 0], done[gi, 1, half] + xchain[g, 1], g)
        g = 2 * (1 - pairing) + gi
        renorm_comp(ochain[gi, 0] + xchain[g, 0], ochain[gi, 1] + xchain[g, 1], g)

    for ch in range(2):
        for way in (RIGHT, LEFT):
            for k in range(3):
                @pl.when(n_can_send(way, k))
                def _():
                    wait_for(nall.at[0, ch], n_s.at[way, k, ch])

            for t in range(2):
                wait_for(xchain.at[0, ch], x_s.at[way, t, ch])

        for t in range(2):
            @pl.when((s == 1) | (s == 2))
            def _():
                wait_for(ochain.at[0, ch], o_s.at[RIGHT, t, ch])
                wait_for(ochain.at[0, ch], o_s.at[LEFT, t, ch])

    for inv in range(2):
        wait_for(rows.at[inv, :, pl.ds(0, 15), 0], f_s.at[inv])
        wait_for(rows.at[inv, :, :, core], c_s.at[inv])
        wait_for(part.at[inv, :, :, pl.ds(0, 15)], k_s.at[inv])
    wait_for(coef.at[:, pl.ds(0, 15)], ip_s)

    @pl.when((s == 0) | (s == 3))
    def _():
        wait_for(coef.at[:, 0], iz_s)


def on_device(normal_ops, integrals, site_terms, basis):
    sem = pltpu.SemaphoreType.DMA
    vmem = pl.BlockSpec(memory_space=pltpu.VMEM)
    return pl.pallas_call(
        kernel,
        name="renormalize",
        out_shape=(
            jax.ShapeDtypeStruct((2, 2, 4, 128, 128), F32),
            jax.ShapeDtypeStruct((2, 1, 4, 128, 128), F32),
        ),
        in_specs=[vmem, vmem, pl.BlockSpec(memory_space=pltpu.SMEM), pl.BlockSpec(memory_space=pl.ANY)],
        out_specs=(vmem, vmem),
        scratch_shapes=[
            pltpu.VMEM((2, 4, 512, 128), F32),
            pltpu.VMEM((4, 256, 512), BF16),
            pltpu.VMEM((4, 256, 512), BF16),
            pltpu.VMEM((4, 2, 2, 16, 8, 128), F32),
            pltpu.VMEM((2, 2, 16, 2, 2, 8, 128), F32),
            pltpu.VMEM((2, 16, 8, 128), F32),
            pltpu.VMEM((2, 2, 2, 16, 8, 128), F32),
            pltpu.VMEM((2, 2, 2, 16, 8, 128), F32),
            pltpu.VMEM((2, 2, 16, 8, 128), F32),
            pltpu.VMEM((4, 2, 16, 8, 128), F32),
            sem,
            sem((2, 3, 2)), sem((2, 3, 2)),
            sem((2,)), sem((2,)),
            sem((2,)), sem((2,)),
            sem, sem, sem, sem,
            sem((2,)), sem((2,)),
            sem((2, 2, 2)), sem((2, 2)),
            sem((2, 2, 2)), sem((2, 2, 2)),
        ],
        compiler_params=pltpu.CompilerParams(
            collective_id=0, has_side_effects=True, vmem_limit_bytes=32 * 2**20
        ),
    )(normal_ops.reshape(2, 2, 16, 8, 128), integrals, site_terms, basis)


def solution(mesh):
    placed = (
        P(None, "pair", None, "sec"),
        P(None, "pair", None),
        P(None, "pair", None, None),
        P(None, None, None, "sec"),
    )
    return jax.shard_map(
        on_device,
        mesh=mesh,
        in_specs=placed,
        out_specs=(P(None, "pair", None, None, "sec"), P(None, "pair", None, None, "sec")),
        check_vma=False,
    )
```

profile of v0, /device:TPU:2, one launch (start us, length us, event | category | flops | bytes accessed | tf_op | source)
XLA Modules:
  0.0 58.8 jit_solution(7212511935837750488)
XLA Ops:
  0.6 0.0 copy-start
  0.6 1.6 %copy-done = f32[2,4,512,128]{3,2,1,0:T(8,128)S(1)} copy-done((f32[2,4,512,128]{3,2,1,0:T(8,128)S(1)}, f32[2,4,512,128]{3,2,1,0:T(8,128)}, u32[]{:S(2)}) %copy-start) | copy-done | bytes 2097176
  2.2 0.0 copy-start.1
  2.2 0.9 %copy-done.1 = f32[2,2,128,128]{3,2,1,0:T(8,128)S(1)} copy-done((f32[2,2,128,128]{3,2,1,0:T(8,128)S(1)}, f32[2,2,128,128]{3,2,1,0:T(8,128)}, u32[]{:S(2)}) %copy-start.1) | copy-done | bytes 262168
  3.2 0.0 copy-start.2
  3.2 0.7 %copy-done.2 = f32[2,1,4,4]{3,2,1,0:T(4,128)S(1)} copy-done((f32[2,1,4,4]{3,2,1,0:T(4,128)S(1)}, f32[2,1,4,4]{3,2,1,0:T(4,128)}, u32[]{:S(2)}) %copy-start.2) | copy-done | bytes 152
  3.9 0.0 copy-start.3
  3.9 0.7 %copy-done.3 = f32[2,1,128]{2,1,0:T(1,128)S(1)} copy-done((f32[2,1,128]{2,1,0:T(1,128)S(1)}, f32[2,1,128]{2,1,0:T(1,128)}, u32[]{:S(2)}) %copy-start.3) | copy-done | bytes 1048
  4.5 52.5 %renormalize.1 = (f32[2,2,4,128,128]{4,3,2,1,0:T(8,128)S(1)}, f32[2,1,4,128,128]{4,3,2,1,0:T(8,128)S(1)}) custom-call(f32[2,2,16,8,128]{4,3,2,1,0:T(8,128)S(1)} %bitcast.1, f32[2,1,128]{2,1,0:T(1,128)S(1)} %copy-done.3, f32[2,1,4,4]{3,2,1,0:T(4,128)S(1)} %copy-done.2, f32[2,4,512,128]{3,2,1,0:T(8,128)S(1)} %copy-done), custom_call_target="tpu_custom_call" | custom-call | tf_op jit(solution)/shard_map/renormalize/pallas_call | solution.py:369
  57.0 1.0 %copy.8 = f32[2,2,4,128,128]{4,3,2,1,0:T(8,128)} copy(f32[2,2,4,128,128]{4,3,2,1,0:T(8,128)S(1)} %get-tuple-element.4) | data formatting | bytes 2097152
  58.0 0.8 %copy.9 = f32[2,1,4,128,128]{4,3,2,1,0:T(8,128)} copy(f32[2,1,4,128,128]{4,3,2,1,0:T(8,128)S(1)} %get-tuple-element.5) | data formatting | bytes 1048576
Async XLA Ops:
  0.6 1.6 %copy-start = (f32[2,4,512,128]{3,2,1,0:T(8,128)S(1)}, f32[2,4,512,128]{3,2,1,0:T(8,128)}, u32[]{:S(2)}) copy-start(f32[2,4,512,128]{3,2,1,0:T(8,128)} %b_hbm.1) | copy-start | bytes 6291460
  2.2 0.9 %copy-start.1 = (f32[2,2,128,128]{3,2,1,0:T(8,128)S(1)}, f32[2,2,128,128]{3,2,1,0:T(8,128)}, u32[]{:S(2)}) copy-start(f32[2,2,128,128]{3,2,1,0:T(8,128)} %param.4) | copy-start | bytes 786436
  3.2 0.7 %copy-start.2 = (f32[2,1,4,4]{3,2,1,0:T(4,128)S(1)}, f32[2,1,4,4]{3,2,1,0:T(4,128)}, u32[]{:S(2)}) copy-start(f32[2,1,4,4]{3,2,1,0:T(4,128)} %t_ref.1) | copy-start | bytes 388
  3.9 0.7 %copy-start.3 = (f32[2,1,128]{2,1,0:T(1,128)S(1)}, f32[2,1,128]{2,1,0:T(1,128)}, u32[]{:S(2)}) copy-start(f32[2,1,128]{2,1,0:T(1,128)} %i_ref.1) | copy-start | bytes 3076
where the time goes:
time: 59 us; the launch traced here: 58.8 us
  Pallas kernels  52.5 us (89%)
  local copies, waits for them, and re-layouts  5.66 us (10%)
  between operations  0.65 us (1%)
    pallas_call x1, Pallas kernels, on_device(): pl.pallas_call(kernel, name='renormalize', out_shape=(jax.ShapeDtypeStruc...  52.5 us
    unnamed x10, local copies, waits for them, and re-layouts  5.66 us

commit v1 on v0

v1 whole, which is shorter than its diff:
```python
import jax
import jax.numpy as jnp
from jax import lax
from jax.experimental import pallas as pl
from jax.experimental.pallas import tpu as pltpu
from jax.sharding import PartitionSpec as P

MESH = pl.DeviceIdType.MESH
F32 = jnp.float32
BF16 = jnp.bfloat16
RIGHT, LEFT = 0, 1


def split(x):
    high = x.astype(BF16)
    return high, (x - high.astype(F32)).astype(BF16)


def kernel(
    n_hbm, i_hbm, t_hbm, b_hbm, on_ref, oc_ref,
    i_ref, t_ref, bas, bhi, blo, nall, rows, coef, part, done, ochain, xchain,
    in_sem, n_s, n_r, f_s, f_r, c_s, c_r, iz_s, iz_r, ip_s, ip_r, k_s, k_r, oo_s, of_s, o_r, xo_s, xf_s, x_r,
):
    p = lax.axis_index("pair")
    s = lax.axis_index("sec")
    half = p // 32
    chip = (p // 2) % 16
    core = p % 2
    pairing = s // 2
    odd = s % 2

    def on_chip(q):
        return (half * 32 + q * 2 + core, s)

    mate = (p - core + (1 - core), s)
    z_up = ((p + 32 * ((s + 1) // 4)) % 64, (s + 1) % 4)
    z_down = ((p + 32 * ((4 - s) // 4)) % 64, (s + 3) % 4)
    z_to = (z_up, z_down)
    edge = (s == 0) | (s == 3)
    edge_beyond = ((p + 32) % 64, 3 * (s // 2))
    inner_beyond = ((p + 32) % 64, 1 + s // 2)

    def remote(src, dst, send, recv, to):
        return pltpu.make_async_remote_copy(
            src_ref=src, dst_ref=dst, send_sem=send, recv_sem=recv, device_id=to, device_id_type=MESH
        )

    def wait_for(ref, sem):
        pltpu.make_async_copy(ref, ref, sem).wait()

    copies = [
        pltpu.make_async_copy(src, dst, in_sem.at[k])
        for k, (src, dst) in enumerate(((i_hbm, i_ref), (n_hbm, nall.at[s]), (t_hbm, t_ref), (b_hbm, bas)))
    ]
    for copy in copies:
        copy.start()

    barrier = pltpu.get_barrier_semaphore()

    @pl.loop(1, 16)
    def _(d):
        pl.semaphore_signal(barrier, inc=1, device_id=on_chip((chip + d) % 16), device_id_type=MESH)

    for to in (mate, z_up, z_down):
        pl.semaphore_signal(barrier, inc=1, device_id=to, device_id_type=MESH)

    @pl.when(edge)
    def _():
        pl.semaphore_signal(barrier, inc=1, device_id=inner_beyond, device_id_type=MESH)

    copies[0].wait()
    re = jnp.broadcast_to(i_ref[0], (8, 128))
    im = jnp.broadcast_to(i_ref[1], (8, 128))
    re_t, im_t = pltpu.roll(re, 64, 1), pltpu.roll(im, 64, 1)
    low = lax.broadcasted_iota(jnp.int32, (8, 128), 1) < 64
    row = lax.broadcasted_iota(jnp.int32, (8, 128), 0)
    tile = jnp.where(
        row == 0,
        jnp.where(low, re, -im_t),
        jnp.where(
            row == 1,
            jnp.where(low, im, re_t),
            jnp.where(row == 2, jnp.where(low, re_t, -im), jnp.where(low, im_t, re)),
        ),
    )
    coef[half, chip] = tile
    copies[1].wait()
    pl.semaphore_wait(barrier, jnp.where(edge, 18, 19))


    @pl.when(s == 3)
    def _():
        remote(coef.at[half, chip], coef.at[half, chip], iz_s, iz_r, z_up).start()

    @pl.when(s == 0)
    def _():
        remote(coef.at[half, chip], coef.at[half, chip], iz_s, iz_r, z_down).start()

    def n_slot(way, k):
        return s - k if way == RIGHT else s + k

    def n_can_send(way, k):
        return (s < 3) & (s >= k) if way == RIGHT else (s > 0) & (s + k <= 3)

    def n_can_recv(way, k):
        return s - 1 >= k if way == RIGHT else s + 1 + k <= 3

    def n_piece(slot, c):
        return nall.at[slot, c // 2, c % 2]

    def n_send(way, k, c):
        @pl.when(n_can_send(way, k))
        def _():
            piece = n_piece(n_slot(way, k), c)
            remote(piece, piece, n_s.at[way, k, c], n_r.at[way, k, c], z_to[way]).start()

    def n_wait(way, k, c):
        @pl.when(n_can_recv(way, k))
        def _():
            wait_for(n_piece(n_slot(way, k + 1), c), n_r.at[way, k, c])

    for c in range(4):
        for way in (RIGHT, LEFT):
            n_send(way, 0, c)

    def forward(inv, slot, r):
        @pl.loop(1, 16)
        def _(d):
            q = (chip + d) % 16
            remote(nall.at[slot, r, :, q], rows.at[inv, r, chip, core], f_s.at[inv], f_r.at[inv], on_chip(q)).start()

        rows[inv, r, chip, core] = nall[slot, r, :, chip]

    def forward_whole(inv, slot):
        @pl.loop(1, 16)
        def _(d):
            q = (chip + d) % 16
            remote(nall.at[slot, :, :, q], rows.at[inv, :, chip, core], f_s.at[inv], f_r.at[inv], on_chip(q)).start()

        rows[inv, :, chip, core] = nall[slot, :, :, chip]

    forward_whole(0, s)

    wait_for(coef.at[1 - half, chip], iz_r)

    @pl.when(s == 0)
    def _():
        remote(coef.at[1 - half, chip], coef.at[1 - half, chip], iz_s, iz_r, z_up).start()

    @pl.when(s == 3)
    def _():
        remote(coef.at[1 - half, chip], coef.at[1 - half, chip], iz_s, iz_r, z_down).start()

    @pl.loop(1, 16)
    def _(d):
        remote(coef.at[:, chip], coef.at[:, chip], ip_s, ip_r, on_chip((chip + d) % 16)).start()

    copies[3].wait()
    for g in range(4):
        for r in range(2):
            for a in range(4):
                high, rest = split(bas[r, a, pl.ds(128 * g, 128)])
                bhi[g, pl.ds(128 * r, 128), pl.ds(128 * a, 128)] = high
                blo[g, pl.ds(128 * r, 128), pl.ds(128 * a, 128)] = rest

    def product(real, imag, g):
        top = split(jnp.concatenate([real, -imag], axis=1))
        bottom = split(jnp.concatenate([imag, real], axis=1))
        out = []
        for high, rest in (top, bottom):
            for pair in range(2):
                cols = pl.ds(256 * pair, 256)
                b_high, b_rest = bhi[g, :, cols], blo[g, :, cols]
                dot = lambda x, y: jnp.dot(x, y, preferred_element_type=F32)
                out.append(dot(high, b_high) + (dot(high, b_rest) + dot(rest, b_high)))
        return out

    def renorm_normal(src, g, first=False):
        for j in range(2):
            real = src[0, j].reshape(128, 128)
            imag = src[1, j].reshape(128, 128)
            res = product(real, imag, g)
            for r in range(2):
                for a in range(4):
                    value = res[2 * r + a // 2][:, 128 * (a % 2) : 128 * (a % 2) + 128]
                    if first:
                        on_ref[r, j, a] = value
                    else:
                        on_ref[r, j, a] += value

    def renorm_comp(real, imag, g):
        res = product(real.reshape(128, 128), imag.reshape(128, 128), g)
        for r in range(2):
            for a in range(4):
                oc_ref[r, 0, a] += res[2 * r + a // 2][:, 128 * (a % 2) : 128 * (a % 2) + 128]

    renorm_normal(nall.at[s], s, first=True)
    copies[2].wait()

    for a in range(4):
        real = jnp.zeros((128, 128), F32)
        imag = jnp.zeros((128, 128), F32)
        for b in range(4):
            t_re, t_im = t_ref[0, 0, a, b], t_ref[1, 0, a, b]
            b_re, b_im = bas[0, b, pl.ds(0, 128)], bas[1, b, pl.ds(0, 128)]
            real += t_re * b_re - t_im * b_im
            imag += t_re * b_im + t_im * b_re
        oc_ref[0, 0, a] = real
        oc_ref[1, 0, a] = imag

    def swap(inv):
        wait_for(rows.at[inv, :, pl.ds(0, 15), 0], f_r.at[inv])
        remote(rows.at[inv, :, :, core], rows.at[inv, :, :, core], c_s.at[inv], c_r.at[inv], mate).start()

    def complementary(inv):
        wait_for(rows.at[inv, :, :, 1 - core], c_r.at[inv])
        flat = rows.at[inv].reshape(1024, 128)
        table = coef.reshape(256, 128)
        lines = [table[pl.ds(i, 32, stride=8), :] for i in range(4)]
        left = jnp.concatenate(
            [jnp.where(half == 0, lines[0], lines[2]), jnp.where(half == 0, lines[1], lines[3])], axis=0
        )
        out = part.at[inv].reshape(512, 128)
        for i in range(8):
            res = jnp.dot(left, flat[pl.ds(i, 128, stride=8), :], preferred_element_type=F32, precision=lax.Precision.HIGHEST)
            out[pl.ds(i, 64, stride=8), :] = res

    def back(inv, gi):
        @pl.loop(1, 16)
        def _(d):
            q = (chip + d) % 16
            remote(part.at[inv, :, :, q], done.at[gi, :, :, chip], k_s.at[inv], k_r.at[inv], on_chip(q)).start()

        done[gi, :, :, chip] = part[inv, :, :, chip]

    def wait_back(inv, gi):
        wait_for(done.at[gi, :, :, pl.ds(0, 15)], k_r.at[inv])

    def done_piece(gi, c, whose):
        return done.at[gi, c // 2, whose, pl.ds(8 * (c % 2), 8)]

    def x_piece(g, c):
        return xchain.at[g, c // 2, pl.ds(8 * (c % 2), 8)]

    def o_piece(gi, c):
        return ochain.at[gi, c // 2, pl.ds(8 * (c % 2), 8)]

    def mirrored(v, g):
        return g if v < 2 else 3 - g

    def originate(v, t):
        gi = (v + t) % 2
        g = 2 * (v // 2) + gi
        for c in range(4):
            if v in (0, 3):
                to = z_to[LEFT if v == 0 else RIGHT]
                remote(done_piece(gi, c, 1 - half), x_piece(g, c), xo_s.at[gi, c], x_r.at[g, c], to).start()
            else:
                if t == 0:
                    remote(done_piece(gi, c, 1 - half), x_piece(g, c), xo_s.at[gi, c], x_r.at[g, c], edge_beyond).start()
                to = z_to[RIGHT if v == 1 else LEFT]
                remote(done_piece(gi, c, half), o_piece(gi, c), oo_s.at[gi, c], o_r.at[gi, c], to).start()

    def x_take(v, g, on):
        g = mirrored(v, g)
        for c in range(4):
            wait_for(x_piece(g, c), x_r.at[g, c])
            if on is not None:
                to = z_to[RIGHT if (on == "inward") == (v < 2) else LEFT]
                remote(x_piece(g, c), x_piece(g, c), xf_s.at[g, c], x_r.at[g, c], to).start()

    def o_take(v, g):
        gi = mirrored(v, g) % 2
        for c in range(4):
            wait_for(o_piece(gi, c), o_r.at[gi, c])
            if v in (1, 2):
                to = z_to[LEFT if v == 1 else RIGHT]
                remote(o_piece(gi, c), o_piece(gi, c), of_s.at[gi, c], o_r.at[gi, c], to).start()

    def each(step):
        for v in range(4):
            @pl.when(s == v)
            def _(v=v):
                step(v, v in (0, 3))

    def early(v, at_edge):
        if at_edge:
            x_take(v, 3, "inward")
            o_take(v, 2)
        else:
            o_take(v, 2)
            x_take(v, 3, "inward")

    def late_first(v, at_edge):
        if at_edge:
            x_take(v, 1, "inward")
            x_take(v, 2, "inward")
        else:
            x_take(v, 0, "outward")
            o_take(v, 3)

    def late_second(v, at_edge):
        x_take(v, 0 if at_edge else 1, None)

    def late_third(v, at_edge):
        if at_edge:
            o_take(v, 3)
        else:
            x_take(v, 2, None)

    def from_end(g):
        return jnp.where(s < 2, g, 3 - g)

    def comp_own(g):
        g = from_end(g)
        gi = g % 2
        renorm_comp(done[gi, 0, half] + xchain[g, 0], done[gi, 1, half] + xchain[g, 1], g)

    def comp_other(g):
        g = from_end(g)
        gi = g % 2
        renorm_comp(ochain[gi, 0] + xchain[g, 0], ochain[gi, 1] + xchain[g, 1], g)

    def n_step(k, pieces):
        for c in pieces:
            for way in (RIGHT, LEFT):
                n_wait(way, k, c)
                if k < 2:
                    n_send(way, k + 1, c)

    def n_renorm(k):
        for way in (RIGHT, LEFT):
            @pl.when(n_can_recv(way, k))
            def _():
                slot = n_slot(way, k + 1)
                renorm_normal(nall.at[slot], slot)

    other = s + 1 - 2 * odd
    n_step(0, (0, 1))
    forward(1, other, 0)
    swap(0)
    n_step(0, (2, 3))
    forward(1, other, 1)
    wait_for(coef.at[:, pl.ds(0, 15)], ip_r)
    complementary(0)
    back(0, odd)
    n_renorm(0)
    swap(1)
    n_step(1, range(4))
    wait_back(0, odd)
    each(lambda v, at_edge: originate(v, 0))
    complementary(1)
    back(1, 1 - odd)
    n_renorm(1)
    each(early)
    wait_back(1, 1 - odd)
    each(lambda v, at_edge: originate(v, 1))
    each(late_first)
    n_step(2, range(4))
    n_renorm(2)
    comp_own(jnp.where(edge, 1, 0))
    comp_other(jnp.where(edge, 2, 3))
    each(late_second)
    comp_own(jnp.where(edge, 0, 1))
    each(late_third)
    comp_other(jnp.where(edge, 3, 2))

    for c in range(4):
        for way in (RIGHT, LEFT):
            for k in range(3):
                @pl.when(n_can_send(way, k))
                def _():
                    wait_for(n_piece(0, c), n_s.at[way, k, c])

    def sent(v, at_edge):
        for c in range(4):
            for gi in range(2):
                if at_edge or gi == v % 2:
                    wait_for(x_piece(0, c), xo_s.at[gi, c])
                if not at_edge:
                    wait_for(o_piece(0, c), oo_s.at[gi, c])
                    wait_for(o_piece(0, c), of_s.at[gi, c])
            for g in (1, 2, 3) if at_edge else (0, 3):
                wait_for(x_piece(0, c), xf_s.at[mirrored(v, g), c])

    each(sent)

    for inv in range(2):
        wait_for(rows.at[inv, :, pl.ds(0, 15), 0], f_s.at[inv])
        wait_for(rows.at[inv, :, :, core], c_s.at[inv])
        wait_for(part.at[inv, :, :, pl.ds(0, 15)], k_s.at[inv])
    wait_for(coef.at[:, pl.ds(0, 15)], ip_s)

    @pl.when((s == 0) | (s == 3))
    def _():
        wait_for(coef.at[:, 0], iz_s)


def on_device(normal_ops, integrals, site_terms, basis):
    inputs = (normal_ops.reshape(2, 2, 16, 8, 128), integrals, site_terms, basis)
    sem = pltpu.SemaphoreType.DMA
    vmem = pl.BlockSpec(memory_space=pltpu.VMEM)
    return pl.pallas_call(
        kernel,
        name="renormalize",
        out_shape=(
            jax.ShapeDtypeStruct((2, 2, 4, 128, 128), F32),
            jax.ShapeDtypeStruct((2, 1, 4, 128, 128), F32),
        ),
        in_specs=[pl.BlockSpec(memory_space=pltpu.HBM)] * 4,
        out_specs=(vmem, vmem),
        scratch_shapes=[
            pltpu.VMEM((2, 1, 128), F32),
            pltpu.SMEM((2, 1, 4, 4), F32),
            pltpu.VMEM((2, 4, 512, 128), F32),
            pltpu.VMEM((4, 256, 512), BF16),
            pltpu.VMEM((4, 256, 512), BF16),
            pltpu.VMEM((4, 2, 2, 16, 8, 128), F32),
            pltpu.VMEM((2, 2, 16, 2, 2, 8, 128), F32),
            pltpu.VMEM((2, 16, 8, 128), F32),
            pltpu.VMEM((2, 2, 2, 16, 8, 128), F32),
            pltpu.VMEM((2, 2, 2, 16, 8, 128), F32),
            pltpu.VMEM((2, 2, 16, 8, 128), F32),
            pltpu.VMEM((4, 2, 16, 8, 128), F32),
            sem((4,)),
            sem((2, 3, 4)), sem((2, 3, 4)),
            sem((2,)), sem((2,)),
            sem((2,)), sem((2,)),
            sem, sem, sem, sem,
            sem((2,)), sem((2,)),
            sem((2, 4)), sem((2, 4)), sem((2, 4)),
            sem((2, 4)), sem((4, 4)), sem((4, 4)),
        ],
        compiler_params=pltpu.CompilerParams(
            collective_id=0, has_side_effects=True, vmem_limit_bytes=32 * 2**20
        ),
    )(*(pltpu.with_memory_space_constraint(x, pltpu.HBM) for x in inputs))


def solution(mesh):
    placed = (
        P(None, "pair", None, "sec"),
        P(None, "pair", None),
        P(None, "pair", None, None),
        P(None, None, None, "sec"),
    )
    return jax.shard_map(
        on_device,
        mesh=mesh,
        in_specs=placed,
        out_specs=(P(None, "pair", None, None, "sec"), P(None, "pair", None, None, "sec")),
        check_vma=False,
    )
```

time: 59 us -> 50.1 us (0.85)
  the two profiles are of different devices: /device:TPU:2 before, /device:TPU:32 now
where the time goes in v1:
time: 50.1 us; the launch traced here: 50 us
  Pallas kernels  47.6 us (95%)
  local copies, waits for them, and re-layouts  1.77 us (4%)
  between operations  0.64 us (1%)
    pallas_call x1, Pallas kernels, on_device(): pl.pallas_call(kernel, name='renormalize', out_shape=(jax.ShapeDtypeStruc...  47.6 us
    unnamed x2, local copies, waits for them, and re-layouts  1.77 us

profile of v1, /device:TPU:32, one launch (start us, length us, event | category | flops | bytes accessed | tf_op | source)
XLA Modules:
  0.0 50.0 jit_solution(7972061608193464922)
XLA Ops:
  0.6 47.6 %renormalize.1 = (f32[2,2,4,128,128]{4,3,2,1,0:T(8,128)S(1)}, f32[2,1,4,128,128]{4,3,2,1,0:T(8,128)S(1)}) custom-call(f32[2,2,16,8,128]{4,3,2,1,0:T(8,128)} %bitcast.1, f32[2,1,128]{2,1,0:T(1,128)} %i_hbm.1, f32[2,1,4,4]{3,2,1,0:T(4,128)} %t_hbm.1, f32[2,4,512,128]{3,2,1,0:T(8,128)} %b_hbm.1), custom_call_target="tpu_custom_call" | custom-call | tf_op jit(solution)/shard_map/renormalize/pallas_call | solution.py:403
  48.2 1.0 %copy.8 = f32[2,2,4,128,128]{4,3,2,1,0:T(8,128)} copy(f32[2,2,4,128,128]{4,3,2,1,0:T(8,128)S(1)} %get-tuple-element.4) | data formatting | bytes 2097152
  49.2 0.8 %copy.9 = f32[2,1,4,128,128]{4,3,2,1,0:T(8,128)} copy(f32[2,1,4,128,128]{4,3,2,1,0:T(8,128)S(1)} %get-tuple-element.5) | data formatting | bytes 1048576

commit v2 on v1

v2 whole, which is shorter than its diff:
```python
import jax
import jax.numpy as jnp
from jax import lax
from jax.experimental import pallas as pl
from jax.experimental.pallas import tpu as pltpu
from jax.sharding import PartitionSpec as P

MESH = pl.DeviceIdType.MESH
F32 = jnp.float32
BF16 = jnp.bfloat16
RIGHT, LEFT = 0, 1
OFFSETS = sorted(
    ((y, x) for y in range(4) for x in range(4) if (y, x) != (0, 0)),
    key=lambda o: -(min(o[0], 4 - o[0]) + min(o[1], 4 - o[1])),
)


def split(x):
    high = x.astype(BF16)
    return high, (x - high.astype(F32)).astype(BF16)


def kernel(
    n_hbm, i_hbm, t_hbm, b_hbm, on_ref, oc_ref,
    i_ref, t_ref, bas, bcat, nall, rows, coef, part, done, ochain, xchain,
    in_sem, n_s, n_r, g_s, g_r, f_s, f_r, c_s, c_r, iz_s, iz_r, ip_s, ip_r, k_s, k_r, oo_s, op_s, op_r, of_s, o_r, xb_s, xo_s, xf_s, x_r, ready,
):
    p = lax.axis_index("pair")
    s = lax.axis_index("sec")
    half = p // 32
    chip = (p // 2) % 16
    core = p % 2
    pairing = s // 2
    odd = s % 2

    chips = [(chip // 4 + y) % 4 * 4 + (chip % 4 + x) % 4 for y, x in OFFSETS]

    other = s + 1 - 2 * odd
    skip = (s + 2) % 4
    inner_neighbour = (p, 3 - s)

    def on_chip(q):
        return (half * 32 + q * 2 + core, s)

    def on_pair(q):
        return (half * 32 + q * 2 + core, other)

    mate = (p - core + (1 - core), s)
    z_up = ((p + 32 * ((s + 1) // 4)) % 64, (s + 1) % 4)
    z_down = ((p + 32 * ((4 - s) // 4)) % 64, (s + 3) % 4)
    z_to = (z_up, z_down)
    edge = (s == 0) | (s == 3)
    beyond = ((p + 32) % 64, s + 1 - 2 * (s % 2))
    second = ((p + 32) % 64, (s + 2) % 4)

    def remote(src, dst, send, recv, to):
        return pltpu.make_async_remote_copy(
            src_ref=src, dst_ref=dst, send_sem=send, recv_sem=recv, device_id=to, device_id_type=MESH
        )

    def wait_for(ref, sem):
        pltpu.make_async_copy(ref, ref, sem).wait()

    copies = [
        pltpu.make_async_copy(src, dst, in_sem.at[k])
        for k, (src, dst) in enumerate(((i_hbm, i_ref), (n_hbm, nall.at[s]), (t_hbm, t_ref), (b_hbm, bas)))
    ]
    for copy in copies:
        copy.start()

    barrier = pltpu.get_barrier_semaphore()

    for to in [on_chip(q) for q in chips] + [beyond, second, (p, skip), z_up, z_down]:
        pl.semaphore_signal(barrier, inc=1, device_id=to, device_id_type=MESH)

    @pl.when(edge)
    def _():
        for q in chips:
            pl.semaphore_signal(barrier, inc=1, device_id=on_pair(q), device_id_type=MESH)

    @pl.when(core == 0)
    def _():
        pl.semaphore_signal(barrier, inc=1, device_id=mate, device_id_type=MESH)

    copies[0].wait()
    re = jnp.broadcast_to(i_ref[0], (8, 128))
    im = jnp.broadcast_to(i_ref[1], (8, 128))
    re_t, im_t = pltpu.roll(re, 64, 1), pltpu.roll(im, 64, 1)
    low = lax.broadcasted_iota(jnp.int32, (8, 128), 1) < 64
    row = lax.broadcasted_iota(jnp.int32, (8, 128), 0)
    tile = jnp.where(
        row == 0,
        jnp.where(low, re, -im_t),
        jnp.where(
            row == 1,
            jnp.where(low, im, re_t),
            jnp.where(row == 2, jnp.where(low, re_t, -im), jnp.where(low, im_t, re)),
        ),
    )
    coef[half, chip] = tile
    copies[1].wait()
    pl.semaphore_wait(barrier, jnp.where(edge, 20, 35) + core)

    @pl.when(core == 1)
    def _():
        pl.semaphore_signal(ready, inc=1, device_id=mate, device_id_type=MESH)


    @pl.when(edge)
    def _():
        remote(coef.at[half, chip], coef.at[half, chip], iz_s, iz_r, second).start()

    @pl.when(s == 3)
    def _():
        remote(coef.at[half, chip], coef.at[half, chip], iz_s, iz_r, z_up).start()

    @pl.when(s == 0)
    def _():
        remote(coef.at[half, chip], coef.at[half, chip], iz_s, iz_r, z_down).start()

    for q in chips:
        remote(nall.at[s, :, :, q], rows.at[0, :, chip, core], f_s.at[0], f_r.at[0], on_chip(q)).start()

    @pl.when(~edge)
    def _():
        for q in chips + [chip]:
            remote(nall.at[s, :, :, q], rows.at[1, :, chip, core], f_s.at[1], f_r.at[1], on_pair(q)).start()

    rows[0, :, chip, core] = nall[s, :, :, chip]

    def n_slot(way, k):
        return s - k if way == RIGHT else s + k

    def n_can_send(way, k):
        if k == 0:
            return s < 2 if way == RIGHT else s > 1
        return (s < 3) & (s >= k) if way == RIGHT else (s > 0) & (s + k <= 3)

    def n_can_recv(way, k):
        if k == 0:
            return ~edge
        return s - 1 >= k if way == RIGHT else s + 1 + k <= 3

    def n_send(way, k, c):
        @pl.when(n_can_send(way, k))
        def _():
            piece = nall.at[n_slot(way, k), c]
            remote(piece, piece, n_s.at[way, k, c], n_r.at[way, k, c], z_to[way]).start()

    def n_step(k):
        for c in range(2):
            for way in (RIGHT, LEFT):
                @pl.when(n_can_recv(way, k))
                def _():
                    wait_for(nall.at[n_slot(way, k + 1), c], n_r.at[way, k, c])

                if k < 2:
                    n_send(way, k + 1, c)

    for c in range(2):
        for way in (RIGHT, LEFT):
            n_send(way, 0, c)

    def give_back():
        for q in chips:
            remote(rows.at[1, :, q, core], nall.at[other, :, :, chip], g_s, g_r, on_chip(q)).start()
        nall[other, :, :, chip] = rows[1, :, chip, core]

    def n_pair():
        wait_for(nall.at[other, :, :, pl.ds(0, 15)], g_r)

    wait_for(coef.at[1 - half, chip], iz_r)
    for q in chips:
        remote(coef.at[:, chip], coef.at[:, chip], ip_s, ip_r, on_chip(q)).start()

    copies[3].wait()
    for g in range(4):
        for r in range(2):
            for a in range(4):
                high, rest = split(bas[r, a, pl.ds(128 * g, 128)])
                for k, value in enumerate((high, high, rest)):
                    bcat[g, pl.ds(256 * k + 128 * r, 128), pl.ds(128 * a, 128)] = value

    def product(real, imag, g):
        left = jnp.concatenate(
            [jnp.concatenate([real, -imag], axis=1), jnp.concatenate([imag, real], axis=1)], axis=0
        )
        high, rest = split(left)
        left = jnp.concatenate([high, rest, high], axis=1)
        return [
            jnp.dot(left, bcat[g, :, pl.ds(256 * pair, 256)], preferred_element_type=F32) for pair in range(2)
        ]

    def renorm_normal(src, g, first=False):
        res = product(src[0].reshape(256, 128), src[1].reshape(256, 128), g)
        for r in range(2):
            for j in range(2):
                for a in range(4):
                    value = res[a // 2][256 * r + 128 * j : 256 * r + 128 * j + 128, 128 * (a % 2) : 128 * (a % 2) + 128]
                    if first:
                        on_ref[r, j, a] = value
                    else:
                        on_ref[r, j, a] += value

    def renorm_comp(real, imag, g):
        res = product(real.reshape(128, 128), imag.reshape(128, 128), g)
        for r in range(2):
            for a in range(4):
                oc_ref[r, 0, a] += res[a // 2][128 * r : 128 * r + 128, 128 * (a % 2) : 128 * (a % 2) + 128]

    def site_part():
        copies[2].wait()
        for a in range(4):
            real = jnp.zeros((128, 128), F32)
            imag = jnp.zeros((128, 128), F32)
            for b in range(4):
                t_re, t_im = t_ref[0, 0, a, b], t_ref[1, 0, a, b]
                b_re, b_im = bas[0, b, pl.ds(0, 128)], bas[1, b, pl.ds(0, 128)]
                real += t_re * b_re - t_im * b_im
                imag += t_re * b_im + t_im * b_re
            oc_ref[0, 0, a] = real
            oc_ref[1, 0, a] = imag

    def swap(inv):
        remote(rows.at[inv, :, :, core], rows.at[inv, :, :, core], c_s.at[inv], c_r.at[inv], mate).start()

    def complementary(inv):
        wait_for(rows.at[inv, :, :, 1 - core], c_r.at[inv])
        flat = rows.at[inv].reshape(1024, 128)
        table = coef.reshape(256, 128)
        lines = [table[pl.ds(i, 32, stride=8), :] for i in range(4)]
        left = jnp.concatenate(
            [jnp.where(half == 0, lines[0], lines[2]), jnp.where(half == 0, lines[1], lines[3])], axis=0
        )
        out = part.at[inv].reshape(512, 128)
        for i in range(8):
            res = jnp.dot(left, flat[pl.ds(i, 128, stride=8), :], preferred_element_type=F32, precision=lax.Precision.HIGHEST)
            out[pl.ds(i, 64, stride=8), :] = res

    def back(inv, gi):
        for q in chips:
            remote(part.at[inv, :, :, q], done.at[gi, :, :, chip], k_s.at[inv], k_r.at[inv], on_chip(q)).start()
        done[gi, :, :, chip] = part[inv, :, :, chip]

    def wait_back(inv, gi):
        wait_for(done.at[gi, :, :, pl.ds(0, 15)], k_r.at[inv])

    def done_piece(gi, c, whose):
        return done.at[gi, c, whose]

    def x_piece(g, c):
        return xchain.at[g, c]

    def o_piece(gi, c):
        return ochain.at[gi, c]

    def mirrored(v, g):
        return g if v < 2 else 3 - g

    def originate(v, t):
        gi = (v + t) % 2
        g = 2 * (v // 2) + gi
        for c in range(2):
            theirs, ours = done_piece(gi, c, 1 - half), done_piece(gi, c, half)
            if v in (0, 3):
                away = z_to[LEFT if v == 0 else RIGHT]
                far = beyond if t == 0 else second
                remote(theirs, x_piece(g, c), xb_s.at[t, c], x_r.at[g, c], far).start()
                if t == 0:
                    remote(ours, o_piece(gi, c), oo_s.at[c], o_r.at[gi, c], (p, skip)).start()
                    remote(ours, ours, op_s.at[c], op_r.at[c], (p, other)).start()
                remote(theirs, x_piece(g, c), xo_s.at[t, c], x_r.at[g, c], away).start()
            elif t == 0:
                remote(theirs, x_piece(g, c), xb_s.at[t, c], x_r.at[g, c], beyond).start()
                remote(ours, o_piece(gi, c), oo_s.at[c], o_r.at[gi, c], inner_neighbour).start()

    def x_take(v, g, on):
        g = mirrored(v, g)
        for c in range(2):
            wait_for(x_piece(g, c), x_r.at[g, c])
            if on is not None:
                to = z_to[RIGHT if (on == "inward") == (v < 2) else LEFT]
                remote(x_piece(g, c), x_piece(g, c), xf_s.at[g, c], x_r.at[g, c], to).start()

    def o_take(v, g):
        gi = mirrored(v, g) % 2
        for c in range(2):
            wait_for(o_piece(gi, c), o_r.at[gi, c])
            if v in (1, 2):
                to = z_to[LEFT if v == 1 else RIGHT]
                remote(o_piece(gi, c), o_piece(gi, c), of_s.at[gi, c], o_r.at[gi, c], to).start()

    def each(step):
        for v in range(4):
            @pl.when(s == v)
            def _(v=v):
                step(v, v in (0, 3))

    def early(v, at_edge):
        if at_edge:
            x_take(v, 3, "inward")
            x_take(v, 1, "inward")
        else:
            o_take(v, 2)
            x_take(v, 0, "outward")
            o_take(v, 3)
            for c in range(2):
                wait_for(done_piece(0, c, half), op_r.at[c])

    def late_first(v, at_edge):
        if at_edge:
            x_take(v, 0, None)
        else:
            x_take(v, 3, None)
            x_take(v, 1, None)

    def late_second(v, at_edge):
        if at_edge:
            o_take(v, 3)

    def late_third(v, at_edge):
        if at_edge:
            o_take(v, 2)
        x_take(v, 2, None)

    def from_end(g):
        return jnp.where(s < 2, g, 3 - g)

    def comp_own(g):
        g = from_end(g)
        gi = g % 2
        renorm_comp(done[gi, 0, half] + xchain[g, 0], done[gi, 1, half] + xchain[g, 1], g)

    def comp_other(g):
        g = from_end(g)
        gi = g % 2
        renorm_comp(ochain[gi, 0] + xchain[g, 0], ochain[gi, 1] + xchain[g, 1], g)

    def n_renorm(k):
        for way in (RIGHT, LEFT):
            @pl.when(n_can_recv(way, k))
            def _():
                slot = n_slot(way, k + 1)
                renorm_normal(nall.at[slot], slot)

    @pl.when(core == 0)
    def _():
        pl.semaphore_wait(ready, 1)

    wait_for(rows.at[0, :, pl.ds(0, 15), 0], f_r.at[0])
    swap(0)
    n_step(0)
    wait_for(coef.at[:, pl.ds(0, 15)], ip_r)
    complementary(0)
    back(0, odd)

    @pl.when(edge)
    def _():
        wait_for(rows.at[1, :, :, 0], f_r.at[1])
        swap(1)
        give_back()
        complementary(1)
        back(1, 1 - odd)

    @pl.when(~edge)
    def _():
        renorm_normal(nall.at[s], s, first=True)
        n_renorm(0)

    wait_back(0, odd)
    each(lambda v, at_edge: originate(v, 0))
    n_step(1)
    site_part()

    @pl.when(edge)
    def _():
        renorm_normal(nall.at[s], s, first=True)
        n_pair()
        renorm_normal(nall.at[other], other)
        wait_back(1, 1 - odd)

    each(lambda v, at_edge: originate(v, 1))
    each(early)
    n_renorm(1)
    comp_own(jnp.where(edge, 1, 0))
    n_step(2)
    n_renorm(2)
    each(late_first)
    comp_own(jnp.where(edge, 0, 1))
    each(late_second)
    comp_other(3)
    each(late_third)
    comp_other(2)

    for c in range(2):
        for way in (RIGHT, LEFT):
            for k in range(3):
                @pl.when(n_can_send(way, k))
                def _():
                    wait_for(nall.at[0, c], n_s.at[way, k, c])

    def sent(v, at_edge):
        for c in range(2):
            wait_for(x_piece(0, c), xb_s.at[0, c])
            wait_for(o_piece(0, c), oo_s.at[c])
            if at_edge:
                wait_for(o_piece(0, c), op_s.at[c])
                wait_for(x_piece(0, c), xb_s.at[1, c])
                for t in range(2):
                    wait_for(x_piece(0, c), xo_s.at[t, c])
                for g in (1, 3):
                    wait_for(x_piece(0, c), xf_s.at[mirrored(v, g), c])
            else:
                for gi in range(2):
                    wait_for(o_piece(0, c), of_s.at[gi, c])
                wait_for(x_piece(0, c), xf_s.at[mirrored(v, 0), c])

    each(sent)

    def sent_exchange(inv):
        wait_for(rows.at[inv, :, :, core], c_s.at[inv])
        wait_for(part.at[inv, :, :, pl.ds(0, 15)], k_s.at[inv])

    wait_for(rows.at[0, :, pl.ds(0, 15), 0], f_s.at[0])
    sent_exchange(0)

    @pl.when(edge)
    def _():
        sent_exchange(1)
        wait_for(nall.at[other, :, :, pl.ds(0, 15)], g_s)

    @pl.when(~edge)
    def _():
        wait_for(rows.at[1, :, :, 0], f_s.at[1])

    wait_for(coef.at[:, pl.ds(0, 15)], ip_s)

    @pl.when((s == 0) | (s == 3))
    def _():
        wait_for(coef.at[:, 0], iz_s)


def on_device(normal_ops, integrals, site_terms, basis):
    inputs = (normal_ops.reshape(2, 2, 16, 8, 128), integrals, site_terms, basis)
    shapes = (
        jax.ShapeDtypeStruct((2, 2, 4, 128, 128), F32),
        jax.ShapeDtypeStruct((2, 1, 4, 128, 128), F32),
    )
    sem = pltpu.SemaphoreType.DMA
    vmem = pl.BlockSpec(memory_space=pltpu.VMEM)
    return pl.pallas_call(
        kernel,
        name="renormalize",
        out_shape=shapes,
        in_specs=[pl.BlockSpec(memory_space=pltpu.HBM)] * 4,
        out_specs=(vmem, vmem),
        scratch_shapes=[
            pltpu.VMEM((2, 1, 128), F32),
            pltpu.SMEM((2, 1, 4, 4), F32),
            pltpu.VMEM((2, 4, 512, 128), F32),
            pltpu.VMEM((4, 768, 512), BF16),
            pltpu.VMEM((4, 2, 2, 16, 8, 128), F32),
            pltpu.VMEM((2, 2, 16, 2, 2, 8, 128), F32),
            pltpu.VMEM((2, 16, 8, 128), F32),
            pltpu.VMEM((2, 2, 2, 16, 8, 128), F32),
            pltpu.VMEM((2, 2, 2, 16, 8, 128), F32),
            pltpu.VMEM((2, 2, 16, 8, 128), F32),
            pltpu.VMEM((4, 2, 16, 8, 128), F32),
            sem((4,)),
            sem((2, 3, 2)), sem((2, 3, 2)),
            sem, sem,
            sem((2,)), sem((2,)),
            sem((2,)), sem((2,)),
            sem, sem, sem, sem,
            sem((2,)), sem((2,)),
            sem((2,)), sem((2,)), sem((2,)), sem((2, 2)), sem((2, 2)),
            sem((2, 2)), sem((2, 2)), sem((4, 2)), sem((4, 2)),
            pltpu.SemaphoreType.REGULAR,
        ],
        compiler_params=pltpu.CompilerParams(
            collective_id=0, has_side_effects=True, vmem_limit_bytes=32 * 2**20
        ),
    )(*(pltpu.with_memory_space_constraint(x, pltpu.HBM) for x in inputs))


def solution(mesh):
    placed = (
        P(None, "pair", None, "sec"),
        P(None, "pair", None),
        P(None, "pair", None, None),
        P(None, None, None, "sec"),
    )
    return jax.shard_map(
        on_device,
        mesh=mesh,
        in_specs=placed,
        out_specs=(P(None, "pair", None, None, "sec"), P(None, "pair", None, None, "sec")),
        check_vma=False,
    )
```

time: 50.1 us -> 47.7 us (0.952)
  Pallas kernels: 47.6 us -> 45.2 us
    pallas_call x1, Pallas kernels: 47.6 us -> 45.2 us  [on_device(): pl.pallas_call(kernel, name='renormalize', out_shape=shapes, in_specs=[pl...]
where the time goes in v2:
time: 47.7 us; the launch traced here: 47.6 us
  Pallas kernels  45.2 us (95%)
  local copies, waits for them, and re-layouts  1.77 us (4%)
  between operations  0.64 us (1%)
    pallas_call x1, Pallas kernels, on_device(): pl.pallas_call(kernel, name='renormalize', out_shape=shapes, in_specs=[pl...  45.2 us
    unnamed x2, local copies, waits for them, and re-layouts  1.77 us

profile of v2, /device:TPU:32, one launch (start us, length us, event | category | flops | bytes accessed | tf_op | source)
XLA Modules:
  0.0 47.6 jit_solution(12703758502232316689)
XLA Ops:
  0.6 45.2 %renormalize.1 = (f32[2,2,4,128,128]{4,3,2,1,0:T(8,128)S(1)}, f32[2,1,4,128,128]{4,3,2,1,0:T(8,128)S(1)}) custom-call(f32[2,2,16,8,128]{4,3,2,1,0:T(8,128)} %bitcast.1, f32[2,1,128]{2,1,0:T(1,128)} %i_hbm.1, f32[2,1,4,4]{3,2,1,0:T(4,128)} %t_hbm.1, f32[2,4,512,128]{3,2,1,0:T(8,128)} %b_hbm.1), custom_call_target="tpu_custom_call" | custom-call | tf_op jit(solution)/shard_map/renormalize/pallas_call | solution.py:451
  45.9 1.0 %copy.8 = f32[2,2,4,128,128]{4,3,2,1,0:T(8,128)} copy(f32[2,2,4,128,128]{4,3,2,1,0:T(8,128)S(1)} %get-tuple-element.4) | data formatting | bytes 2097152
  46.8 0.8 %copy.9 = f32[2,1,4,128,128]{4,3,2,1,0:T(8,128)} copy(f32[2,1,4,128,128]{4,3,2,1,0:T(8,128)S(1)} %get-tuple-element.5) | data formatting | bytes 1048576

commit v3 on v2

--- a/solution.py
+++ b/solution.py
@@ -23,7 +23,7 @@
 def kernel(
     n_hbm, i_hbm, t_hbm, b_hbm, on_ref, oc_ref,
     i_ref, t_ref, bas, bcat, nall, rows, coef, part, done, ochain, xchain,
-    in_sem, n_s, n_r, g_s, g_r, f_s, f_r, c_s, c_r, iz_s, iz_r, ip_s, ip_r, k_s, k_r, oo_s, op_s, op_r, of_s, o_r, xb_s, xo_s, xf_s, x_r, ready,
+    in_sem, n_s, n_r, g_s, g_r, f_s, f_r, c_s, c_r, iz_s, iz_r, ip_s, ip_r, k_s, k_r, oo_s, op_s, op_r, of_s, o_r, xb_s, xo_s, xf_s, xi_s, x_r, ready,
 ):
     p = lax.axis_index("pair")
     s = lax.axis_index("sec")
@@ -264,23 +264,23 @@
             theirs, ours = done_piece(gi, c, 1 - half), done_piece(gi, c, half)
             if v in (0, 3):
                 away = z_to[LEFT if v == 0 else RIGHT]
-                far = beyond if t == 0 else second
-                remote(theirs, x_piece(g, c), xb_s.at[t, c], x_r.at[g, c], far).start()
                 if t == 0:
-                    remote(ours, o_piece(gi, c), oo_s.at[c], o_r.at[gi, c], (p, skip)).start()
+                    remote(theirs, x_piece(g, c), xb_s.at[t, c], x_r.at[g, c], beyond).start()
                     remote(ours, ours, op_s.at[c], op_r.at[c], (p, other)).start()
                 remote(theirs, x_piece(g, c), xo_s.at[t, c], x_r.at[g, c], away).start()
             elif t == 0:
                 remote(theirs, x_piece(g, c), xb_s.at[t, c], x_r.at[g, c], beyond).start()
                 remote(ours, o_piece(gi, c), oo_s.at[c], o_r.at[gi, c], inner_neighbour).start()
 
-    def x_take(v, g, on):
+    def x_take(v, g, outward=(), inward=()):
         g = mirrored(v, g)
         for c in range(2):
-            wait_for(x_piece(g, c), x_r.at[g, c])
-            if on is not None:
-                to = z_to[RIGHT if (on == "inward") == (v < 2) else LEFT]
-                remote(x_piece(g, c), x_piece(g, c), xf_s.at[g, c], x_r.at[g, c], to).start()
+            piece = x_piece(g, c)
+            wait_for(piece, x_r.at[g, c])
+            if c in outward:
+                remote(piece, piece, xf_s.at[g, c], x_r.at[g, c], z_to[LEFT if v < 2 else RIGHT]).start()
+            if c in inward:
+                remote(piece, piece, xi_s.at[g, c], x_r.at[g, c], z_to[RIGHT if v < 2 else LEFT]).start()
 
     def o_take(v, g):
         gi = mirrored(v, g) % 2
@@ -290,6 +290,13 @@
                 to = z_to[LEFT if v == 1 else RIGHT]
                 remote(o_piece(gi, c), o_piece(gi, c), of_s.at[gi, c], o_r.at[gi, c], to).start()
 
+    def edge_take(v):
+        gi = mirrored(v, 0) % 2
+        for c in range(2):
+            piece = done_piece(gi, c, half)
+            wait_for(piece, op_r.at[c])
+            remote(piece, o_piece(gi, c), op_s.at[c], o_r.at[gi, c], inner_neighbour).start()
+
     def each(step):
         for v in range(4):
             @pl.when(s == v)
@@ -298,21 +305,21 @@
 
     def early(v, at_edge):
         if at_edge:
-            x_take(v, 3, "inward")
-            x_take(v, 1, "inward")
+            x_take(v, 1, inward=(0, 1))
+            x_take(v, 3, inward=(0,))
         else:
             o_take(v, 2)
-            x_take(v, 0, "outward")
+            edge_take(v)
+            x_take(v, 0, outward=(0, 1), inward=(1,))
             o_take(v, 3)
-            for c in range(2):
-                wait_for(done_piece(0, c, half), op_r.at[c])
 
     def late_first(v, at_edge):
         if at_edge:
-            x_take(v, 0, None)
+            x_take(v, 2, inward=(0, 1))
+            x_take(v, 0)
         else:
-            x_take(v, 3, None)
-            x_take(v, 1, None)
+            x_take(v, 3)
+            x_take(v, 1)
 
     def late_second(v, at_edge):
         if at_edge:
@@ -321,7 +328,8 @@
     def late_third(v, at_edge):
         if at_edge:
             o_take(v, 2)
-        x_take(v, 2, None)
+        else:
+            x_take(v, 2)
 
     def from_end(g):
         return jnp.where(s < 2, g, 3 - g)
@@ -402,18 +410,19 @@
     def sent(v, at_edge):
         for c in range(2):
             wait_for(x_piece(0, c), xb_s.at[0, c])
-            wait_for(o_piece(0, c), oo_s.at[c])
+            wait_for(o_piece(0, c), op_s.at[c])
             if at_edge:
-                wait_for(o_piece(0, c), op_s.at[c])
-                wait_for(x_piece(0, c), xb_s.at[1, c])
                 for t in range(2):
                     wait_for(x_piece(0, c), xo_s.at[t, c])
-                for g in (1, 3):
-                    wait_for(x_piece(0, c), xf_s.at[mirrored(v, g), c])
+                for g in (1, 2, 3) if c == 0 else (1, 2):
+                    wait_for(x_piece(0, c), xi_s.at[mirrored(v, g), c])
             else:
+                wait_for(o_piece(0, c), oo_s.at[c])
                 for gi in range(2):
                     wait_for(o_piece(0, c), of_s.at[gi, c])
                 wait_for(x_piece(0, c), xf_s.at[mirrored(v, 0), c])
+                if c == 1:
+                    wait_for(x_piece(0, c), xi_s.at[mirrored(v, 0), c])
 
     each(sent)
 
@@ -474,7 +483,7 @@
             sem, sem, sem, sem,
             sem((2,)), sem((2,)),
             sem((2,)), sem((2,)), sem((2,)), sem((2, 2)), sem((2, 2)),
-            sem((2, 2)), sem((2, 2)), sem((4, 2)), sem((4, 2)),
+            sem((2, 2)), sem((2, 2)), sem((4, 2)), sem((4, 2)), sem((4, 2)),
             pltpu.SemaphoreType.REGULAR,
         ],
         compiler_params=pltpu.CompilerParams(

time: 47.7 us -> 45.8 us (0.960)
  Pallas kernels: 45.2 us -> 43.3 us
    pallas_call x1, Pallas kernels: 45.2 us -> 43.3 us  [on_device(): pl.pallas_call(kernel, name='renormalize', out_shape=shapes, in_specs=[pl...]
where the time goes in v3:
time: 45.8 us; the launch traced here: 45.7 us
  Pallas kernels  43.3 us (95%)
  local copies, waits for them, and re-layouts  1.77 us (4%)
  between operations  0.64 us (1%)
    pallas_call x1, Pallas kernels, on_device(): pl.pallas_call(kernel, name='renormalize', out_shape=shapes, in_specs=[pl...  43.3 us
    unnamed x2, local copies, waits for them, and re-layouts  1.77 us

profile of v3, /device:TPU:32, one launch (start us, length us, event | category | flops | bytes accessed | tf_op | source)
XLA Modules:
  0.0 45.7 jit_solution(8239710653202434903)
XLA Ops:
  0.6 43.3 %renormalize.1 = (f32[2,2,4,128,128]{4,3,2,1,0:T(8,128)S(1)}, f32[2,1,4,128,128]{4,3,2,1,0:T(8,128)S(1)}) custom-call(f32[2,2,16,8,128]{4,3,2,1,0:T(8,128)} %bitcast.1, f32[2,1,128]{2,1,0:T(1,128)} %i_hbm.1, f32[2,1,4,4]{3,2,1,0:T(4,128)} %t_hbm.1, f32[2,4,512,128]{3,2,1,0:T(8,128)} %b_hbm.1), custom_call_target="tpu_custom_call" | custom-call | tf_op jit(solution)/shard_map/renormalize/pallas_call | solution.py:460
  43.9 1.0 %copy.8 = f32[2,2,4,128,128]{4,3,2,1,0:T(8,128)} copy(f32[2,2,4,128,128]{4,3,2,1,0:T(8,128)S(1)} %get-tuple-element.4) | data formatting | bytes 2097152
  44.9 0.8 %copy.9 = f32[2,1,4,128,128]{4,3,2,1,0:T(8,128)} copy(f32[2,1,4,128,128]{4,3,2,1,0:T(8,128)S(1)} %get-tuple-element.5) | data formatting | bytes 1048576

commit v4 on v3

--- a/solution.py
+++ b/solution.py
@@ -36,7 +36,6 @@
     chips = [(chip // 4 + y) % 4 * 4 + (chip % 4 + x) % 4 for y, x in OFFSETS]
 
     other = s + 1 - 2 * odd
-    skip = (s + 2) % 4
     inner_neighbour = (p, 3 - s)
 
     def on_chip(q):
@@ -70,7 +69,7 @@
 
     barrier = pltpu.get_barrier_semaphore()
 
-    for to in [on_chip(q) for q in chips] + [beyond, second, (p, skip), z_up, z_down]:
+    for to in [on_chip(q) for q in chips] + [beyond, second, z_up, z_down]:
         pl.semaphore_signal(barrier, inc=1, device_id=to, device_id_type=MESH)
 
     @pl.when(edge)
@@ -99,7 +98,7 @@
     )
     coef[half, chip] = tile
     copies[1].wait()
-    pl.semaphore_wait(barrier, jnp.where(edge, 20, 35) + core)
+    pl.semaphore_wait(barrier, jnp.where(edge, 19, 34) + core)
 
     @pl.when(core == 1)
     def _():
@@ -232,9 +231,13 @@
         left = jnp.concatenate(
             [jnp.where(half == 0, lines[0], lines[2]), jnp.where(half == 0, lines[1], lines[3])], axis=0
         )
+        high, rest = split(left)
+        left3 = jnp.concatenate([high, rest, high], axis=1)
         out = part.at[inv].reshape(512, 128)
         for i in range(8):
-            res = jnp.dot(left, flat[pl.ds(i, 128, stride=8), :], preferred_element_type=F32, precision=lax.Precision.HIGHEST)
+            x_high, x_rest = split(flat[pl.ds(i, 128, stride=8), :])
+            right = jnp.concatenate([x_high, x_high, x_rest], axis=0)
+            res = jnp.dot(left3, right, preferred_element_type=F32)
             out[pl.ds(i, 64, stride=8), :] = res
 
     def back(inv, gi):

time: 45.8 us -> 45.5 us (level)
  no operation moved by 1% of the time
where the time goes in v4:
time: 45.5 us; the launch traced here: 45.4 us
  Pallas kernels  43 us (95%)
  local copies, waits for them, and re-layouts  1.77 us (4%)
  between operations  0.64 us (1%)
    pallas_call x1, Pallas kernels, on_device(): pl.pallas_call(kernel, name='renormalize', out_shape=shapes, in_specs=[pl...  43 us
    unnamed x2, local copies, waits for them, and re-layouts  1.77 us

profile of v4, /device:TPU:32, one launch (start us, length us, event | category | flops | bytes accessed | tf_op | source)
XLA Modules:
  0.0 45.4 jit_solution(1958641350202601086)
XLA Ops:
  0.6 43.0 %renormalize.1 = (f32[2,2,4,128,128]{4,3,2,1,0:T(8,128)S(1)}, f32[2,1,4,128,128]{4,3,2,1,0:T(8,128)S(1)}) custom-call(f32[2,2,16,8,128]{4,3,2,1,0:T(8,128)} %bitcast.1, f32[2,1,128]{2,1,0:T(1,128)} %i_hbm.1, f32[2,1,4,4]{3,2,1,0:T(4,128)} %t_hbm.1, f32[2,4,512,128]{3,2,1,0:T(8,128)} %b_hbm.1), custom_call_target="tpu_custom_call" | custom-call | tf_op jit(solution)/shard_map/renormalize/pallas_call | solution.py:463
  43.6 1.0 %copy.8 = f32[2,2,4,128,128]{4,3,2,1,0:T(8,128)} copy(f32[2,2,4,128,128]{4,3,2,1,0:T(8,128)S(1)} %get-tuple-element.4) | data formatting | bytes 2097152
  44.6 0.8 %copy.9 = f32[2,1,4,128,128]{4,3,2,1,0:T(8,128)} copy(f32[2,1,4,128,128]{4,3,2,1,0:T(8,128)S(1)} %get-tuple-element.5) | data formatting | bytes 1048576

commit v5 on v4

--- a/solution.py
+++ b/solution.py
@@ -311,8 +311,8 @@
             x_take(v, 1, inward=(0, 1))
             x_take(v, 3, inward=(0,))
         else:
+            edge_take(v)
             o_take(v, 2)
-            edge_take(v)
             x_take(v, 0, outward=(0, 1), inward=(1,))
             o_take(v, 3)
 
@@ -326,11 +326,11 @@
 
     def late_second(v, at_edge):
         if at_edge:
-            o_take(v, 3)
+            o_take(v, 2)
 
     def late_third(v, at_edge):
         if at_edge:
-            o_take(v, 2)
+            o_take(v, 3)
         else:
             x_take(v, 2)
 
@@ -399,9 +399,9 @@
     each(late_first)
     comp_own(jnp.where(edge, 0, 1))
     each(late_second)
-    comp_other(3)
+    comp_other(jnp.where(edge, 2, 3))
     each(late_third)
-    comp_other(2)
+    comp_other(jnp.where(edge, 3, 2))
 
     for c in range(2):
         for way in (RIGHT, LEFT):

time: 45.5 us -> 45.5 us (level)
  no operation moved by 1% of the time
where the time goes in v5:
time: 45.5 us; the launch traced here: 45.4 us
  Pallas kernels  43 us (95%)
  local copies, waits for them, and re-layouts  1.77 us (4%)
  between operations  0.64 us (1%)
    pallas_call x1, Pallas kernels, on_device(): pl.pallas_call(kernel, name='renormalize', out_shape=shapes, in_specs=[pl...  43 us
    unnamed x2, local copies, waits for them, and re-layouts  1.77 us

profile of v5, /device:TPU:32, one launch (start us, length us, event | category | flops | bytes accessed | tf_op | source)
XLA Modules:
  0.0 45.4 jit_solution(18049930850071425714)
XLA Ops:
  0.6 43.0 %renormalize.1 = (f32[2,2,4,128,128]{4,3,2,1,0:T(8,128)S(1)}, f32[2,1,4,128,128]{4,3,2,1,0:T(8,128)S(1)}) custom-call(f32[2,2,16,8,128]{4,3,2,1,0:T(8,128)} %bitcast.1, f32[2,1,128]{2,1,0:T(1,128)} %i_hbm.1, f32[2,1,4,4]{3,2,1,0:T(4,128)} %t_hbm.1, f32[2,4,512,128]{3,2,1,0:T(8,128)} %b_hbm.1), custom_call_target="tpu_custom_call" | custom-call | tf_op jit(solution)/shard_map/renormalize/pallas_call | solution.py:463
  43.6 1.0 %copy.8 = f32[2,2,4,128,128]{4,3,2,1,0:T(8,128)} copy(f32[2,2,4,128,128]{4,3,2,1,0:T(8,128)S(1)} %get-tuple-element.4) | data formatting | bytes 2097152
  44.6 0.8 %copy.9 = f32[2,1,4,128,128]{4,3,2,1,0:T(8,128)} copy(f32[2,1,4,128,128]{4,3,2,1,0:T(8,128)S(1)} %get-tuple-element.5) | data formatting | bytes 1048576
